TPU v7x, 256 devices: a whole 4x4x8 slice. The times are simulated.
256 devices in a mesh: ctx: 32 (over z, y), ch: 8 (over x, core).
Axes of the slice: x: 4, y: 4, z: 8, core: 2. Of those that a mesh axis runs over, the one named last changes fastest.
Arguments:
- queries: bfloat16 [8192, 4096], P('ctx', 'ch'), may hold values from -6 to 6
- keys: bfloat16 [8192, 4096], P('ctx', 'ch'), may hold values from -6 to 6
- values: bfloat16 [8192, 4096], P('ctx', 'ch'), may hold values from -6 to 6
- long_filter: float32 [8192, 4096], P('ctx', 'ch'), may hold values from -1.05 to 1.05
- short_filters: float32 [3, 3, 4096], P(None, None, 'ch'), may hold values from -3.6 to 3.6
- skip: float32 [4096], P('ch'), may hold values from -1 to 1
- w_out: bfloat16 [4096, 8192], P('ch'), may hold values from -0.09375 to 0.09375
- d_out: bfloat16 [8192, 8192], P('ctx', 'ch'), may hold values from -6 to 6
Outputs:
- d_queries: bfloat16 [8192, 4096], P('ctx', 'ch')
- d_keys: bfloat16 [8192, 4096], P('ctx', 'ch')
- d_values: bfloat16 [8192, 4096], P('ctx', 'ch')
- d_long: float32 [8192, 4096], P('ctx', 'ch')
- d_short: float32 [3, 3, 4096], P(None, None, 'ch')
- d_skip: float32 [4096], P('ch')
All inputs are finite; a program needn't handle non-finite values.
Results may differ from a plain program's by a relative error of at most 0.0049.
Values may be sent and summed in bfloat16 or wider, within the bound.
No kernel may reach another device: no remote copies, remote signals or barrier semaphores. Data moves between devices by JAX's collectives and lax.ppermute only.
A program may use at most 128 MiB of HBM per device.

v0:
```python
import math

import jax
import jax.numpy as jnp
from jax import lax
from jax.sharding import PartitionSpec as P


def passed_along(block, axis, distance):
    devices = range(lax.axis_size(axis))
    route = [(i - distance, i) for i in devices if i - distance in devices]
    return lax.ppermute(block, axis, route)


def phases(left_index, right_index, modulus):
    product = left_index[:, None] * right_index[None, :] % modulus
    angle = product.astype(jnp.float32) * (2.0 * math.pi / modulus)
    return (jnp.cos(angle), jnp.sin(angle))


def mat_apply(table, data, form):
    return jnp.einsum(form, table, data, precision=lax.Precision.HIGHEST)


def forward_full(regrouped, ctx_size, position, block_len, total_len):
    seq_rows = ctx_size * block_len
    coarse = jnp.arange(ctx_size, dtype=jnp.int32)
    freq_coarse = jnp.arange(2 * ctx_size, dtype=jnp.int32)
    coarse_cos, coarse_sin = phases(freq_coarse, coarse, 2 * ctx_size)
    first_real = mat_apply(coarse_cos, regrouped, "ka,sabc->skbc")
    first_imag = -mat_apply(coarse_sin, regrouped, "ka,sabc->skbc")
    fine_global = position * block_len + jnp.arange(block_len, dtype=jnp.int32)
    twist_cos, twist_sin = phases(freq_coarse, fine_global, total_len)
    twist_cos = twist_cos[None, :, :, None]
    twist_sin = twist_sin[None, :, :, None]
    second_real = first_real * twist_cos + first_imag * twist_sin
    second_imag = first_imag * twist_cos - first_real * twist_sin
    moved = lax.all_to_all(
        jnp.stack([second_real, second_imag], axis=1),
        "ctx",
        split_axis=2,
        concat_axis=3,
        tiled=True,
    )
    fine_index = jnp.arange(seq_rows, dtype=jnp.int32)
    fine_cos, fine_sin = phases(fine_index, fine_index, seq_rows)
    moved_real = moved[:, 0]
    moved_imag = moved[:, 1]
    spec_real = mat_apply(fine_cos, moved_real, "kb,smbc->smkc") + mat_apply(
        fine_sin, moved_imag, "kb,smbc->smkc"
    )
    spec_imag = mat_apply(fine_cos, moved_imag, "kb,smbc->smkc") - mat_apply(
        fine_sin, moved_real, "kb,smbc->smkc"
    )
    return (spec_real, spec_imag)


def inverse_full(spec_real, spec_imag, ctx_size, position, block_len, total_len):
    seq_rows = spec_real.shape[2]
    fine_index = jnp.arange(seq_rows, dtype=jnp.int32)
    fine_cos, fine_sin = phases(fine_index, fine_index, seq_rows)
    back_real = mat_apply(fine_cos, spec_real, "bk,smkc->smbc") - mat_apply(
        fine_sin, spec_imag, "bk,smkc->smbc"
    )
    back_imag = mat_apply(fine_cos, spec_imag, "bk,smkc->smbc") + mat_apply(
        fine_sin, spec_real, "bk,smkc->smbc"
    )
    returned = lax.all_to_all(
        jnp.stack([back_real, back_imag], axis=1), "ctx", split_axis=3, concat_axis=2, tiled=True
    )
    part_real = returned[:, 0]
    part_imag = returned[:, 1]
    freq_coarse = jnp.arange(2 * ctx_size, dtype=jnp.int32)
    fine_global = position * block_len + jnp.arange(block_len, dtype=jnp.int32)
    twist_cos, twist_sin = phases(freq_coarse, fine_global, total_len)
    twist_cos = twist_cos[None, :, :, None]
    twist_sin = twist_sin[None, :, :, None]
    turned_real = part_real * twist_cos - part_imag * twist_sin
    turned_imag = part_imag * twist_cos + part_real * twist_sin
    coarse = jnp.arange(ctx_size, dtype=jnp.int32)
    coarse_cos, coarse_sin = phases(coarse, freq_coarse, 2 * ctx_size)
    result_real = mat_apply(coarse_cos, turned_real, "ak,skbc->sabc") - mat_apply(
        coarse_sin, turned_imag, "ak,skbc->sabc"
    )
    result_imag = mat_apply(coarse_cos, turned_imag, "ak,skbc->sabc") + mat_apply(
        coarse_sin, turned_real, "ak,skbc->sabc"
    )
    return (result_real / total_len, result_imag / total_len)


def per_device(queries, keys, values, long_filter, short_filters, skip, w_out, d_out):
    ctx_size = lax.axis_size("ctx")
    position = lax.axis_index("ctx")
    seq_rows = queries.shape[0]
    width = queries.shape[1]
    block_len = seq_rows // ctx_size
    total_len = 2 * ctx_size * seq_rows
    tap_count = short_filters.shape[1]
    rim_width = tap_count - 1
    streams = jnp.stack([queries, keys, values])
    before = passed_along(streams[:, seq_rows - rim_width :, :], "ctx", 1)
    extended = jnp.concatenate([before, streams], axis=1).astype(jnp.float32)
    filtered = jnp.zeros((3, seq_rows, width), jnp.float32)
    for j in range(tap_count):
        filtered = (
            filtered
            + short_filters[:, j, None, :]
            * extended[:, rim_width - j : rim_width - j + seq_rows, :]
        )
    mixed = filtered[1] * filtered[2]
    accumulated = lax.dot_general(
        lax.all_gather(d_out, "ch", axis=1, tiled=True),
        w_out,
        (((1,), (1,)), ((), ())),
        preferred_element_type=jnp.float32,
    )
    grad_o = lax.optimization_barrier(accumulated.astype(jnp.bfloat16)).astype(jnp.float32)
    grad_y = grad_o * filtered[0]
    signals = jnp.stack([mixed, long_filter, grad_y])
    regrouped = lax.all_to_all(signals[:, None], "ctx", split_axis=2, concat_axis=1, tiled=True)
    spec_real, spec_imag = forward_full(regrouped, ctx_size, position, block_len, total_len)
    mix_re, mix_im = (spec_real[0], spec_imag[0])
    fil_re, fil_im = (spec_real[1], spec_imag[1])
    grad_re, grad_im = (spec_real[2], spec_imag[2])
    out_re = mix_re * fil_re - mix_im * fil_im
    out_im = mix_re * fil_im + mix_im * fil_re
    back_re = grad_re * fil_re + grad_im * fil_im
    back_im = grad_im * fil_re - grad_re * fil_im
    corr_re = grad_re * mix_re + grad_im * mix_im
    corr_im = grad_im * mix_re - grad_re * mix_im
    result_real, result_imag = inverse_full(
        jnp.stack([out_re, back_re, corr_re]),
        jnp.stack([out_im, back_im, corr_im]),
        ctx_size,
        position,
        block_len,
        total_len,
    )
    timed = lax.all_to_all(result_real, "ctx", split_axis=1, concat_axis=2, tiled=True).reshape(
        3, seq_rows, width
    )
    conv_y = timed[0]
    conv_back = timed[1]
    d_long = timed[2]
    y_full = conv_y + skip[None, :] * mixed
    grad_mixed = conv_back + skip[None, :] * grad_y
    grads = jnp.stack([grad_o * y_full, grad_mixed * filtered[2], grad_mixed * filtered[1]])
    after = passed_along(grads[:, :rim_width, :], "ctx", -1)
    grads_ext = jnp.concatenate([grads, after], axis=1)
    stream_grads = jnp.zeros((3, seq_rows, width), jnp.float32)
    tap_terms = []
    for j in range(tap_count):
        stream_grads = (
            stream_grads + short_filters[:, j, None, :] * grads_ext[:, j : j + seq_rows, :]
        )
        tap_terms.append(
            jnp.sum(grads * extended[:, rim_width - j : rim_width - j + seq_rows, :], axis=1)
        )
    short_terms = jnp.stack(tap_terms, axis=1)
    skip_term = jnp.sum(grad_y * mixed, axis=0)
    d_short, d_skip = lax.psum((short_terms, skip_term), "ctx")
    return (
        stream_grads[0].astype(jnp.bfloat16),
        stream_grads[1].astype(jnp.bfloat16),
        stream_grads[2].astype(jnp.bfloat16),
        d_long,
        d_short,
        d_skip,
    )


def solution(mesh):
    in_specs = (
        P("ctx", "ch"),
        P("ctx", "ch"),
        P("ctx", "ch"),
        P("ctx", "ch"),
        P(None, None, "ch"),
        P("ch"),
        P("ch", None),
        P("ctx", "ch"),
    )
    out_specs = (
        P("ctx", "ch"),
        P("ctx", "ch"),
        P("ctx", "ch"),
        P("ctx", "ch"),
        P(None, None, "ch"),
        P("ch"),
    )
    return jax.shard_map(
        per_device, mesh=mesh, in_specs=in_specs, out_specs=out_specs, check_vma=False
    )
```

profile of v0, /device:TPU:24, one launch (start us, length us, event | category | flops | bytes accessed | tf_op | source)
XLA Modules:
  0.0 694.0 jit_solution(1200529167491770491)
XLA Ops:
  7.2 0.0 all-gather.2.cloned.1.call-start
  7.2 0.7 all-gather.2.cloned.1.call-update
  7.9 0.7 pad_maximum_fusion.15
  8.6 3.5 collective-permute-start
  12.1 0.9 fusion.147
  13.0 1.1 collective-permute-done
  14.2 1.3 maximum_convert_fusion
  15.5 0.5 multiply_add_fusion
  16.0 0.9 slice_multiply_fusion.2
  16.9 30.3 %all-gather.2.cloned.1.call-done = bf16[256,8192]{1,0:T(8,128)(2,1)} async-done(((bf16[256,1024]{1,0:T(8,128)(2,1)}), bf16[256,8192]{1,0:T(8,128)(2,1)}) %all-gather.2.cloned.1.call-update) | async-done | bytes 4194320 | tf_op jit(solution)/shard_map/all_gather | solution.py:112
  47.2 0.0 copy-start
  47.2 0.0 copy-start.1
  47.2 7.1 %convolution_convert_fusion = bf16[256,512]{1,0:T(8,128)(2,1)S(1)} fusion(bf16[256,8192]{1,0:T(8,128)(2,1)} %all-gather.2.cloned.1.call-done, bf16[512,8192]{1,0:T(8,128)(2,1)} %param.14), kind=kOutput, calls=%fused_computation.60 | convolution fusion | flops 2147614720 | bytes 12845056 | tf_op jit(solution)/shard_map/dot_general | solution.py:111
  54.3 0.1 fusion.146
  54.4 0.0 copy-done
  54.4 0.0 copy-done.1
  54.4 0.1 maximum_bitcast_fusion
  54.5 2.8 copy.56
  57.3 10.3 %all-to-all-start = ((f32[3,1,256,512]{3,1,0,2:T(1,128)}), f32[3,1,256,512]{3,1,0,2:T(1,128)}, u32[]{:S(2)}, u32[]{:S(2)}) async-start(f32[3,1,256,512]{3,1,0,2:T(1,128)} %copy.56), calls=%async_computation | async-start | bytes 3145728 | tf_op jit(solution)/shard_map/all_to_all | solution.py:120
  67.7 0.1 fusion.93
  67.8 38.8 %all-to-all-done = f32[3,1,256,512]{3,1,0,2:T(1,128)} async-done(((f32[3,1,256,512]{3,1,0,2:T(1,128)}), f32[3,1,256,512]{3,1,0,2:T(1,128)}, u32[]{:S(2)}, u32[]{:S(2)}) %all-to-all-start) | async-done | bytes 1572896 | tf_op jit(solution)/shard_map/all_to_all | solution.py:120
  106.6 1.6 copy.98
  108.1 4.0 fusion.29
  112.1 4.9 fusion.1
  117.1 1.2 pad_maximum_fusion
  118.3 4.0 copy.60
  122.4 145.7 %all_to_all.57 = f32[3,2,64,8,512]{4,3,0,1,2:T(8,128)S(1)} all-to-all(f32[3,2,64,8,512]{4,3,0,1,2:T(8,128)S(1)} %copy.60), channel_id=1, replica_groups=mesh['ctx'=32,'ch'=8] {'ctx'}, dimensions={2} | all-to-all | bytes 12582912 | tf_op jit(solution)/shard_map/all_to_all | solution.py:38
  268.1 1.0 copy.96
  269.1 6.3 fusion.12
  275.4 6.5 fusion.13
  281.9 6.4 subtract_bitcast_fusion.1
  288.3 6.7 add_bitcast_fusion.1
  295.0 0.4 multiply_add_fusion.3
  295.4 0.4 multiply_subtract_fusion.2
  295.9 3.7 fusion.16
  299.6 3.7 fusion.17
  303.3 4.0 subtract_bitcast_fusion
  307.3 3.9 add_bitcast_fusion
  311.2 3.4 pad_maximum_fusion.1
  314.6 10.3 %copy.65 = f32[3,2,2,256,512]{4,2,0,1,3:T(2,128)} copy(f32[3,2,2,256,512]{3,4,2,0,1:T(8,128)} %pad_maximum_fusion.1) | data formatting | bytes 12582912 | tf_op jit(solution)/shard_map/stack | solution.py:69
  325.0 144.6 %all_to_all.58 = f32[3,2,2,256,512]{4,2,0,1,3:T(2,128)S(1)} all-to-all(f32[3,2,2,256,512]{4,2,0,1,3:T(2,128)} %copy.65), channel_id=1, replica_groups=mesh['ctx'=32,'ch'=8] {'ctx'}, dimensions={3} | all-to-all | bytes 12582912 | tf_op jit(solution)/shard_map/all_to_all | solution.py:68
  469.6 4.6 copy.97
  474.2 10.3 %copy.67 = f32[3,2,32,2,8,512]{5,3,2,4,0,1:T(2,128)} copy(f32[3,2,32,2,8,512]{5,4,2,3,1,0:T(8,128)} %bitcast.217) | data formatting | bytes 12582912 | tf_op jit(solution)/shard_map/all_to_all | solution.py:68
  484.5 8.5 %all_to_all.51 = f32[3,2,64,8,512]{4,2,3,0,1:T(8,128)} reshape(f32[3,2,32,2,8,512]{5,3,2,4,0,1:T(2,128)} %copy.67) | data formatting | bytes 12582912 | tf_op jit(solution)/shard_map/all_to_all | solution.py:68
  493.0 4.5 fusion.4
  497.4 4.6 multiply_bitcast_fusion
  502.0 0.0 copy-start.2
  502.0 0.9 copy.68
  502.9 43.3 %all_to_all.59 = f32[3,32,8,512]{3,2,0,1:T(8,128)S(1)} all-to-all(f32[3,32,8,512]{3,2,0,1:T(8,128)S(1)} %copy.68), channel_id=1, replica_groups=mesh['ctx'=32,'ch'=8] {'ctx'}, dimensions={1} | all-to-all | bytes 3145728 | tf_op jit(solution)/shard_map/all_to_all | solution.py:139
  546.2 0.0 copy-done.2
  546.2 0.4 fusion.33
  546.6 0.1 pad_maximum_fusion.13
  546.7 2.8 collective-permute-start.1
  549.5 0.8 slice_bitcast_fusion.16
  550.3 4.1 collective-permute-done.1
  554.4 0.2 pad_maximum_fusion.12
  554.6 1.1 multiply_reduce_fusion.2
  555.7 129.7 %all-reduce = (f32[3,3,512]{2,0,1:T(4,128)S(1)}, f32[512]{0:T(512)}) all-reduce(f32[3,3,512]{2,0,1:T(4,128)S(1)} %pad_maximum_fusion.14, f32[512]{0:T(512)S(1)} %get-tuple-element.46), channel_id=1, replica_groups=mesh['ctx'=32,'ch'=8] {'ctx'}, use_global_device_ids=true, to_apply=%region_3.4 | all-reduce | flops 5120 | bytes 40960 | tf_op jit(solution)/shard_map/psum | solution.py:161
  685.4 0.6 copy.70
  686.0 0.9 slice_bitcast_fusion.20
  (5 shorter events, 0.0 us)
Async XLA Ops:
  7.2 40.0 %all-gather.2.cloned.1.call-start = ((), (), s32[]{:S(2)}) async-start(), calls=%async_computation.4 | async-start | bytes 4718592 | tf_op jit(solution)/shard_map/all_gather | solution.py:112
  8.6 5.5 collective-permute-start
  47.2 7.2 %copy-start = (f32[1,256,512]{2,1,0:T(8,128)S(1)}, f32[1,256,512]{2,1,0:T(8,128)}, u32[]{:S(2)}) copy-start(f32[1,256,512]{2,1,0:T(8,128)} %slice_multiply_fusion.2) | copy-start | bytes 1572868
  47.2 7.2 %copy-start.1 = (f32[256,512]{1,0:T(8,128)S(1)}, f32[256,512]{1,0:T(8,128)}, u32[]{:S(2)}) copy-start(f32[256,512]{1,0:T(8,128)} %param.11) | copy-start | bytes 1572868
  57.3 49.3 %all-to-all-start = ((f32[3,1,256,512]{3,1,0,2:T(1,128)}), f32[3,1,256,512]{3,1,0,2:T(1,128)}, u32[]{:S(2)}, u32[]{:S(2)}) async-start(f32[3,1,256,512]{3,1,0,2:T(1,128)} %copy.56), calls=%async_computation | async-start | bytes 3145728 | tf_op jit(solution)/shard_map/all_to_all | solution.py:120
  502.0 44.2 %copy-start.2 = (f32[512]{0:T(512)S(1)}, f32[512]{0:T(512)}, u32[]{:S(2)}) copy-start(f32[512]{0:T(512)} %param.13) | copy-start | bytes 6148
  546.7 7.7 %collective-permute-start.1 = (f32[3,2,512]{2,1,0:T(2,128)S(1)}, f32[3,2,512]{2,1,0:T(2,128)S(1)}, u32[]{:S(2)}, u32[]{:S(2)}) collective-permute-start(f32[3,2,512]{2,1,0:T(2,128)S(1)} %slice.149), channel_id=1, source_target_pairs={{8,0},{16,8},{24,16},{32,24},{40,32},{48,40},{56,48},{64,56},{72,6... | collective-permute-start | bytes 36872 | tf_op jit(solution)/shard_map/ppermute | solution.py:12
Sparse Core Ops, SparseCore 0:
  9.8 37.3 all-gather.1
where the time goes:
time: 707 us; the launch traced here: 694 us
  blocking collectives  463 us (65%)
  waiting for transfers between devices  75 us (11%)
  matrix products  66.2 us (9%)
  local copies, waits for them, and re-layouts  47.2 us (7%)
  starting transfers between devices  16.6 us (2%)
  between operations  14.6 us (2%)
  other arithmetic  11 us (2%)
    all_to_all x1, blocking collectives, forward_full(): lax.all_to_all(jnp.stack([second_real, second_imag], axis=1), 'ctx', spli...  146 us
    all_to_all x1, blocking collectives, inverse_full(): lax.all_to_all(jnp.stack([back_real, back_imag], axis=1), 'ctx', split_ax...  145 us
    psum x1, blocking collectives, per_device(): d_short, d_skip = lax.psum((short_terms, skip_term), 'ctx')  130 us
    dot_general x12, matrix products, mat_apply(): return jnp.einsum(form, table, data, precision=lax.Precision.HIGHEST)  59.1 us
    all_to_all x1, blocking collectives, per_device(): lax.all_to_all(result_real, 'ctx', split_axis=1, concat_axis=2, tiled=True)  43.3 us
    all_to_all x1, waiting for transfers between devices, per_device(): lax.all_to_all(signals[:, None], 'ctx', split_axis=2, concat_axis=1, tile...  38.8 us
    all_gather x1, waiting for transfers between devices, per_device(): lax.all_gather(d_out, 'ch', axis=1, tiled=True)  30.3 us
    all_to_all x3, local copies, waits for them, and re-layouts, inverse_full(): lax.all_to_all(jnp.stack([back_real, back_imag], axis=1), 'ctx', split_ax...  23.3 us
  transfers between devices with their start and end apart: 4, of which 4 were waited for; matrix products, arithmetic and copies ran while one was open for 1% of the time, Pallas kernels for 0%

commit v1 on v0

v1 whole, which is shorter than its diff:
```python
import math

import jax
import jax.numpy as jnp
import numpy as np
from jax import lax
from jax.experimental import pallas as pl
from jax.experimental.pallas import tpu as pltpu
from jax.sharding import Mesh, PartitionSpec as P

F32 = jnp.float32
BF16 = jnp.bfloat16
CTX = ("z", "y")
CH = ("x", "core")
SHARDS = 32
ROWS = 256
GROUP = 16
HALF = 8
WIDTH = 512
LENGTH = SHARDS * ROWS
VMEM_LIMIT = 56 * 1024 * 1024


def halves(table):
    high = table.astype(np.float32).astype(jnp.bfloat16)
    low = (table - high.astype(np.float64)).astype(np.float32).astype(jnp.bfloat16)
    return np.asarray(high), np.asarray(low)


def tables():
    coarse = np.arange(SHARDS)
    angle = 2.0 * math.pi * ((np.outer(4 * coarse + 1, coarse) % (4 * SHARDS)) / (4.0 * SHARDS))
    same = np.eye(HALF)
    spread = np.concatenate([np.kron(np.cos(angle), same), np.kron(-np.sin(angle), same)], axis=0)
    fine = np.arange(ROWS)
    angle = 2.0 * math.pi * ((np.outer(fine, fine) % ROWS) / ROWS)
    cos, sin = np.cos(angle), np.sin(angle)
    turn = np.block([[cos, -sin], [sin, cos]])
    twist = 2.0 * math.pi * np.outer(4 * coarse + 1, fine) / (4.0 * LENGTH)
    twist = np.repeat(np.stack([np.cos(twist), np.sin(twist)]), HALF, axis=1).astype(np.float32)
    return (
        *halves(spread),
        *halves(spread.T / LENGTH),
        *halves(turn),
        *halves(turn.T),
        twist,
    )


def dot(left, right):
    return lax.dot_general(left, right, (((1,), (0,)), ((), ())), preferred_element_type=F32)


def split(value):
    high = value.astype(BF16)
    return high, (value - high.astype(F32)).astype(BF16)


def forward(signal, sh, sl, th, tl, twist):
    parts = signal.astype(F32).reshape(SHARDS, 2, HALF, ROWS)
    rows = SHARDS * HALF
    turned = []
    for g in range(2):
        part = parts[:, g].reshape(rows, ROWS).astype(BF16)
        first = dot(sh[...], part) + dot(sl[...], part)
        real, imag = first[:rows], first[rows:]
        turned.append(
            jnp.concatenate(
                [real * twist[0] + imag * twist[1], imag * twist[0] - real * twist[1]], axis=1
            )
        )
    high, low = split(jnp.concatenate(turned, axis=0))
    return dot(high, th[...]) + dot(low, th[...]) + dot(high, tl[...])


def inverse(real, imag, vh, vl, uh, ul, twist):
    high, low = split(jnp.concatenate([real, imag], axis=1))
    back = dot(high, uh[...]) + dot(low, uh[...]) + dot(high, ul[...])
    rows = SHARDS * HALF
    outs = []
    for g in range(2):
        real = back[g * rows : (g + 1) * rows, :ROWS]
        imag = back[g * rows : (g + 1) * rows, ROWS:]
        high, low = split(
            jnp.concatenate(
                [real * twist[0] - imag * twist[1], imag * twist[0] + real * twist[1]], axis=0
            )
        )
        out = dot(vh[...], high) + dot(vh[...], low) + dot(vl[...], high)
        outs.append(out.reshape(SHARDS, HALF, ROWS))
    return jnp.concatenate(outs, axis=1).astype(BF16)


def conv_kernel(moved, sh, sl, vh, vl, th, tl, uh, ul, twist, spec_mix, spec_fil, out):
    mix = forward(moved[:, 0], sh, sl, th, tl, twist)
    fil = forward(moved[:, 1], sh, sl, th, tl, twist)
    spec_mix[...] = mix
    spec_fil[...] = fil
    mix_re, mix_im = mix[:, :ROWS], mix[:, ROWS:]
    fil_re, fil_im = fil[:, :ROWS], fil[:, ROWS:]
    out[...] = inverse(
        mix_re * fil_re - mix_im * fil_im,
        mix_re * fil_im + mix_im * fil_re,
        vh, vl, uh, ul, twist,
    )


def grad_kernel(moved, spec_mix, spec_fil, sh, sl, vh, vl, th, tl, uh, ul, twist, out):
    grad = forward(moved[...], sh, sl, th, tl, twist)
    grad_re, grad_im = grad[:, :ROWS], grad[:, ROWS:]
    for i, spec in enumerate((spec_fil, spec_mix)):
        re, im = spec[:, :ROWS], spec[:, ROWS:]
        out[:, i] = inverse(
            grad_re * re + grad_im * im, grad_im * re - grad_re * im, vh, vl, uh, ul, twist
        )


def mix_kernel(queries, keys, values, before, short, long_filter, send, filtered, ext):
    for s, stream in enumerate((queries, keys, values)):
        ext[0:8, :] = before[s]
        ext[8 : 8 + ROWS, :] = stream[...].astype(F32)
        total = short[s, 0:1, :] * ext[8 : 8 + ROWS, :]
        for j in (1, 2):
            total = total + short[s, j : j + 1, :] * ext[8 - j : 8 - j + ROWS, :]
        filtered[s] = total
    mixed = filtered[1] * filtered[2]
    send[:, 0] = mixed.T.reshape(SHARDS, GROUP, ROWS).astype(BF16)
    send[:, 1] = long_filter[...].T.reshape(SHARDS, GROUP, ROWS).astype(BF16)


def out_proj_kernel(gathered, w_out, filtered, grad_o, send, total):
    step = pl.program_id(0)

    @pl.when(step == 0)
    def _():
        total[...] = jnp.zeros_like(total)

    total[...] += lax.dot_general(
        gathered[0], w_out[...], (((1,), (1,)), ((), ())), preferred_element_type=F32
    )

    @pl.when(step == pl.num_programs(0) - 1)
    def _():
        rounded = total[...].astype(BF16)
        grad_o[...] = rounded
        grad_y = rounded.astype(F32) * filtered[0]
        send[...] = grad_y.T.reshape(SHARDS, GROUP, ROWS).astype(BF16)


def back_kernel(
    grad_o, filtered, conv_y, conv_back, skip, queries, keys, values, before,
    grads, heads, sums, d_long, ext,
):
    grad = grad_o[...].astype(F32)
    mixed = filtered[1] * filtered[2]
    grad_y = grad * filtered[0]
    time_y = conv_y[...].reshape(WIDTH, ROWS).astype(F32).T
    time_back = conv_back[:, 0].reshape(WIDTH, ROWS).astype(F32).T
    d_long[...] = conv_back[:, 1].reshape(WIDTH, ROWS).astype(F32).T
    grad_mixed = time_back + skip[...] * grad_y
    grads[0, 0:ROWS] = grad * (time_y + skip[...] * mixed)
    grads[1, 0:ROWS] = grad_mixed * filtered[2]
    grads[2, 0:ROWS] = grad_mixed * filtered[1]
    sums[...] = jnp.zeros_like(sums)
    for s, stream in enumerate((queries, keys, values)):
        ext[0:8, :] = before[s]
        ext[8 : 8 + ROWS, :] = stream[...].astype(F32)
        heads[s] = grads[s, 0:8]
        for j in range(3):
            sums[3 * s + j : 3 * s + j + 1, :] = jnp.sum(
                grads[s] * ext[8 - j : 8 - j + ROWS, :], axis=0, keepdims=True
            )
    sums[9:10, :] = jnp.sum(grad_y * mixed, axis=0, keepdims=True)


def taps_kernel(grads, after, short, d_queries, d_keys, d_values, ext):
    for s, out in enumerate((d_queries, d_keys, d_values)):
        ext[0:ROWS, :] = grads[s]
        ext[ROWS : ROWS + 8, :] = after[s]
        total = short[s, 0:1, :] * ext[0:ROWS, :]
        for j in (1, 2):
            total = total + short[s, j : j + 1, :] * ext[j : j + ROWS, :]
        out[...] = total.astype(BF16)


def call(kernel, out_shape, *args, scratch=(), name):
    return pl.pallas_call(
        kernel,
        out_shape=out_shape,
        scratch_shapes=scratch,
        compiler_params=pltpu.CompilerParams(vmem_limit_bytes=VMEM_LIMIT),
        name=name,
    )(*args)


def passed_along(block, distance):
    route = [(i - distance, i) for i in range(SHARDS) if 0 <= i - distance < SHARDS]
    return lax.ppermute(block, CTX, route)


def exchange(blocks):
    return lax.all_to_all(blocks, CTX, split_axis=0, concat_axis=0, tiled=True)


def shape(dims, dtype=F32):
    return jax.ShapeDtypeStruct(dims, dtype)


def per_device(queries, keys, values, long_filter, short, skip, w_out, d_out):
    constants = [jnp.asarray(table) for table in tables()]
    gathered = lax.all_gather(d_out, CH, axis=0, tiled=False)
    tails = jnp.stack([queries[ROWS - 2 :], keys[ROWS - 2 :], values[ROWS - 2 :]])
    before = passed_along(tails, 1).astype(F32)
    before = jnp.concatenate([jnp.zeros((3, 6, WIDTH), F32), before], axis=1)
    extended = pltpu.VMEM((ROWS + 8, WIDTH), F32)
    send, filtered = call(
        mix_kernel,
        (shape((SHARDS, 2, GROUP, ROWS), BF16), shape((3, ROWS, WIDTH))),
        queries, keys, values, before, short, long_filter,
        scratch=(extended,),
        name="mix",
    )
    moved = exchange(send)
    spec = shape((2 * SHARDS * HALF, 2 * ROWS))
    spec_mix, spec_fil, conv_y = call(
        conv_kernel,
        (spec, spec, shape((SHARDS, GROUP, ROWS), BF16)),
        moved, *constants,
        name="conv",
    )
    conv_y = exchange(conv_y)
    steps, depth = gathered.shape[0], gathered.shape[2]
    grad_o, grad_send = pl.pallas_call(
        out_proj_kernel,
        grid=(steps,),
        in_specs=[
            pl.BlockSpec((1, ROWS, depth), lambda i: (i, 0, 0)),
            pl.BlockSpec((WIDTH, depth), lambda i: (0, i)),
            pl.BlockSpec((1, ROWS, WIDTH), lambda i: (0, 0, 0)),
        ],
        out_specs=[
            pl.BlockSpec((ROWS, WIDTH), lambda i: (0, 0)),
            pl.BlockSpec((SHARDS, GROUP, ROWS), lambda i: (0, 0, 0)),
        ],
        out_shape=(shape((ROWS, WIDTH), BF16), shape((SHARDS, GROUP, ROWS), BF16)),
        scratch_shapes=[pltpu.VMEM((ROWS, WIDTH), F32)],
        compiler_params=pltpu.CompilerParams(vmem_limit_bytes=VMEM_LIMIT),
        name="out_proj",
    )(gathered, w_out, filtered)
    grad_moved = exchange(grad_send)
    returned = call(
        grad_kernel,
        shape((SHARDS, 2, GROUP, ROWS), BF16),
        grad_moved, spec_mix, spec_fil, *constants,
        name="grad_conv",
    )
    returned = exchange(returned)
    grads, heads, sums, d_long = call(
        back_kernel,
        (shape((3, ROWS, WIDTH)), shape((3, 8, WIDTH)), shape((16, WIDTH)), shape((ROWS, WIDTH))),
        grad_o, filtered, conv_y, returned, skip[None, :], queries, keys, values, before,
        scratch=(extended,),
        name="back",
    )
    after = passed_along(heads, -1)
    shared = exchange(jnp.broadcast_to(sums.astype(BF16)[None], (SHARDS, 16, WIDTH)))
    totals = jnp.sum(shared.astype(F32), axis=0)
    outs = call(
        taps_kernel,
        (shape((ROWS, WIDTH), BF16),) * 3,
        grads, after, short,
        scratch=(extended,),
        name="taps",
    )
    return (*outs, d_long, totals[:9].reshape(3, 3, WIDTH), totals[9])


def solution(mesh):
    fine_mesh = Mesh(mesh.devices.reshape(8, 4, 4, 2), ("z", "y", "x", "core"))
    block = P(CTX, CH)
    in_specs = (block, block, block, block, P(None, None, CH), P(CH), P(CH, None), block)
    out_specs = (block, block, block, block, P(None, None, CH), P(CH))
    return jax.shard_map(
        per_device, mesh=fine_mesh, in_specs=in_specs, out_specs=out_specs, check_vma=False
    )
```

time: 707 us -> 154 us (0.22); the launches traced: 694 us -> 153 us
  blocking collectives: 463 us -> 22.6 us
  matrix products: 66.2 us -> 0 us
  local copies, waits for them, and re-layouts: 47.2 us -> 4.14 us
  waiting for transfers between devices: 75 us -> 36.4 us
  Pallas kernels: 0 us -> 34.8 us
  starting transfers between devices: 16.6 us -> 39.7 us
  other arithmetic: 11 us -> 1.49 us
    all_to_all x3 -> x1, blocking collectives: 334 us -> 22.6 us  [exchange(): return lax.all_to_all(blocks, CTX, split_axis=0, concat_axis=0, tiled=True)]
    psum x1 -> x0, blocking collectives: 130 us -> none  [per_device(): d_short, d_skip = lax.psum((short_terms, skip_term), 'ctx')]
    dot_general x13 -> x0, matrix products: 66.2 us -> none  [the longest x12 59.1 us: mat_apply(): return jnp.einsum(form, table, data, precision=lax.Precision.HIGHEST)]
    pallas_call x0 -> x6, Pallas kernels: none -> 34.8 us  [the longest x5 25.2 us: call(): pl.pallas_call(kernel, out_shape=out_shape, scratch_shapes=scratch, compi...]
    all_to_all x1 -> x4, waiting for transfers between devices: 38.8 us -> 7.71 us  [exchange(): return lax.all_to_all(blocks, CTX, split_axis=0, concat_axis=0, tiled=True)]
    all_to_all x5 -> x0, local copies, waits for them, and re-layouts: 25.9 us -> none  [the longest x3 23.3 us: inverse_full(): lax.all_to_all(jnp.stack([back_real, back_imag], axis=1), 'ctx', split_ax...]
    all_to_all x1 -> x4, starting transfers between devices: 10.3 us -> 33.4 us  [exchange(): return lax.all_to_all(blocks, CTX, split_axis=0, concat_axis=0, tiled=True)]
    all_gather x1, waiting for transfers between devices: 30.3 us -> 16.3 us  [per_device(): gathered = lax.all_gather(d_out, CH, axis=0, tiled=False)]
  transfers between devices with their start and end apart: 4 -> 7, of which waited for: 4 -> 5; matrix products, arithmetic and copies ran while one was open for 1% -> 1% of each run, Pallas kernels for 0% -> 20%
where the time goes in v1:
time: 154 us; the launch traced here: 153 us
  starting transfers between devices  39.7 us (26%)
  waiting for transfers between devices  36.4 us (24%)
  Pallas kernels  34.8 us (23%)
  blocking collectives  22.6 us (15%)
  between operations  14.1 us (9%)
  local copies, waits for them, and re-layouts  4.14 us (3%)
    all_to_all x4, starting transfers between devices, exchange(): return lax.all_to_all(blocks, CTX, split_axis=0, concat_axis=0, tiled=True)  33.4 us
    pallas_call x5, Pallas kernels, call(): pl.pallas_call(kernel, out_shape=out_shape, scratch_shapes=scratch, compi...  25.2 us
    all_to_all x1, blocking collectives, exchange(): return lax.all_to_all(blocks, CTX, split_axis=0, concat_axis=0, tiled=True)  22.6 us
    all_gather x1, waiting for transfers between devices, per_device(): gathered = lax.all_gather(d_out, CH, axis=0, tiled=False)  16.3 us
    ppermute x2, waiting for transfers between devices, passed_along(): return lax.ppermute(block, CTX, route)  11.7 us
    pallas_call x1, Pallas kernels, per_device(): pl.pallas_call(out_proj_kernel, grid=(steps,), in_specs=[pl.BlockSpec((1,...  9.56 us
    all_to_all x4, waiting for transfers between devices, exchange(): return lax.all_to_all(blocks, CTX, split_axis=0, concat_axis=0, tiled=True)  7.71 us
    ppermute x2, starting transfers between devices, passed_along(): return lax.ppermute(block, CTX, route)  6.25 us
  transfers between devices with their start and end apart: 7, of which 5 were waited for; matrix products, arithmetic and copies ran while one was open for 1% of the time, Pallas kernels for 20%

profile of v1, /device:TPU:24, one launch (start us, length us, event | category | flops | bytes accessed | tf_op | source)
XLA Modules:
  0.0 153.1 jit_solution(7296119938329369624)
XLA Ops:
  7.2 0.0 all-gather.3.cloned.1.call-start
  7.2 0.7 all-gather.3.cloned.1.call-update
  7.9 0.7 slice_bitcast_fusion.2
  8.6 0.7 slice_bitcast_fusion
  9.3 3.5 %collective-permute-start = (bf16[3,2,512]{2,1,0:T(2,128)(2,1)S(1)}, bf16[3,2,512]{2,1,0:T(2,128)(2,1)S(1)}, u32[]{:S(2)}, u32[]{:S(2)}) collective-permute-start(bf16[3,2,512]{2,1,0:T(2,128)(2,1)S(1)} %pad_maximum_fusion), channel_id=1, source_target_pairs={{0,8},{8,16},{16,24},{24,32},{32,40},{40,48},{48,56},{56,64},{64,7... | collective-permute-start | bytes 18440 | tf_op jit(solution)/shard_map/ppermute | solution.py:198
  12.8 2.0 %collective-permute-done = bf16[3,2,512]{2,1,0:T(2,128)(2,1)S(1)} collective-permute-done((bf16[3,2,512]{2,1,0:T(2,128)(2,1)S(1)}, bf16[3,2,512]{2,1,0:T(2,128)(2,1)S(1)}, u32[]{:S(2)}, u32[]{:S(2)}) %collective-permute-start) | collective-permute-done | bytes 6176 | tf_op jit(solution)/shard_map/ppermute | solution.py:198
  14.9 0.6 pad_convert_fusion.before
  15.5 3.3 %mix.1 = (bf16[32,2,16,256]{3,2,1,0:T(8,128)(2,1)}, f32[3,256,512]{2,1,0:T(8,128)}) custom-call(bf16[256,512]{1,0:T(8,128)(2,1)} %queries.3, bf16[256,512]{1,0:T(8,128)(2,1)} %keys.3, bf16[256,512]{1,0:T(8,128)(2,1)} %values.3, f32[3,8,512]{2,1,0:T(8,128)} %pad_convert_fusion.before, f32[3,3,512]{2,1,0:T(4,128)} %short.3, f32[256,512]{1,0:T(8,128)} %long_filter.1), custom_call_target="tpu_custom_call" | custom-call | tf_op jit(solution)/shard_map/mix/pallas_call | solution.py:187
  18.8 12.2 %all-to-all-start = ((bf16[32,2,16,256]{3,2,1,0:T(8,128)(2,1)}), bf16[32,2,16,256]{3,2,1,0:T(8,128)(2,1)S(1)}, u32[]{:S(2)}, u32[]{:S(2)}) async-start(bf16[32,2,16,256]{3,2,1,0:T(8,128)(2,1)} %get-tuple-element.22), calls=%async_computation | async-start | bytes 1048576 | tf_op jit(solution)/shard_map/all_to_all | solution.py:202
  31.0 16.3 %all-gather.3.cloned.1.call-done = bf16[2048,1024]{1,0:T(8,128)(2,1)} async-done(((bf16[256,1024]{1,0:T(8,128)(2,1)}), bf16[2048,1024]{1,0:T(8,128)(2,1)}) %all-gather.3.cloned.1.call-update) | async-done | bytes 4194320 | tf_op jit(solution)/shard_map/all_gather | solution.py:211
  47.2 9.6 %out_proj.1 = (bf16[256,512]{1,0:T(8,128)(2,1)}, bf16[32,16,256]{2,1,0:T(8,128)(2,1)}) custom-call(bf16[8,256,1024]{2,1,0:T(8,128)(2,1)} %bitcast.10, bf16[512,8192]{1,0:T(8,128)(2,1)} %w_out.1, f32[3,256,512]{2,1,0:T(8,128)} %get-tuple-element.20.filtered), custom_call_target="tpu_custom_call" | custom-call | tf_op jit(solution)/shard_map/out_proj/pallas_call | solution.py:233
  56.8 0.0 all-to-all-done.moved
  56.8 0.0 copy-start
  56.8 10.1 %all-to-all-start.2 = ((bf16[32,16,256]{2,1,0:T(8,128)(2,1)}), bf16[32,16,256]{2,1,0:T(8,128)(2,1)S(1)}, u32[]{:S(2)}, u32[]{:S(2)}) async-start(bf16[32,16,256]{2,1,0:T(8,128)(2,1)} %get-tuple-element.24), calls=%async_computation.2 | async-start | bytes 524288 | tf_op jit(solution)/shard_map/all_to_all | solution.py:202
  66.9 0.0 copy-done
  66.9 6.9 %conv.1 = (f32[512,512]{1,0:T(8,128)}, f32[512,512]{1,0:T(8,128)}, bf16[32,16,256]{2,1,0:T(8,128)(2,1)}) custom-call(bf16[32,2,16,256]{3,2,1,0:T(8,128)(2,1)} %copy-done, bf16[512,256]{1,0:T(8,128)(2,1)} %constant.23.clone.sh, bf16[512,256]{1,0:T(8,128)(2,1)} %constant.24.clone.sl, bf16[256,512]{1,0:T(8,128)(2,1)} %constant.25.clone.vh, ...), custom_call_target="tpu_custom_call" | custom-call | tf_op jit(solution)/shard_map/conv/pallas_call | solution.py:187
  73.9 4.7 %all-to-all-done.2.moved = bf16[32,16,256]{2,1,0:T(8,128)(2,1)S(1)} async-done(((bf16[32,16,256]{2,1,0:T(8,128)(2,1)}), bf16[32,16,256]{2,1,0:T(8,128)(2,1)S(1)}, u32[]{:S(2)}, u32[]{:S(2)}) %all-to-all-start.2) | async-done | bytes 262176 | tf_op jit(solution)/shard_map/all_to_all | solution.py:202
  78.6 0.0 copy-start.2
  78.6 5.5 %all-to-all-start.1 = ((bf16[32,16,256]{2,1,0:T(8,128)(2,1)}), bf16[32,16,256]{2,1,0:T(8,128)(2,1)S(1)}, u32[]{:S(2)}, u32[]{:S(2)}) async-start(bf16[32,16,256]{2,1,0:T(8,128)(2,1)} %get-tuple-element.23), calls=%async_computation.1 | async-start | bytes 524288 | tf_op jit(solution)/shard_map/all_to_all | solution.py:202
  84.1 0.0 copy-done.2
  84.2 7.7 %grad_conv.1 = bf16[32,2,16,256]{3,2,1,0:T(8,128)(2,1)} custom-call(bf16[32,16,256]{2,1,0:T(8,128)(2,1)} %copy-done.2, f32[512,512]{1,0:T(8,128)} %get-tuple-element.25.spec_mix, f32[512,512]{1,0:T(8,128)} %get-tuple-element.26.spec_fil, bf16[512,256]{1,0:T(8,128)(2,1)} %constant.23.clone.sh, bf16[512,256]{1,0:T(8,128)(2,1)} %constant.24.clone.sl, ...), custom_call_target="tpu_custom_call" | custom-call | tf_op jit(solution)/shard_map/grad_conv/pallas_call | solution.py:187
  91.8 3.0 %all-to-all-done.1.conv_y = bf16[32,16,256]{2,1,0:T(8,128)(2,1)S(1)} async-done(((bf16[32,16,256]{2,1,0:T(8,128)(2,1)}), bf16[32,16,256]{2,1,0:T(8,128)(2,1)S(1)}, u32[]{:S(2)}, u32[]{:S(2)}) %all-to-all-start.1) | async-done | bytes 262176 | tf_op jit(solution)/shard_map/all_to_all | solution.py:202
  94.8 0.0 copy-start.1
  94.8 22.6 %all_to_all.25.conv_back = bf16[32,2,16,256]{3,2,1,0:T(8,128)(2,1)} all-to-all(bf16[32,2,16,256]{3,2,1,0:T(8,128)(2,1)} %grad_conv.1), channel_id=1, replica_groups=mesh['z'=8,'y'=4,'x'=4,'core'=2] {'z','y'}, dimensions={0} | all-to-all | bytes 1048576 | tf_op jit(solution)/shard_map/all_to_all | solution.py:202
  117.4 0.0 copy-done.1
  117.4 4.3 %back.1 = (f32[3,256,512]{2,1,0:T(8,128)}, f32[3,8,512]{2,1,0:T(8,128)}, f32[16,512]{1,0:T(8,128)}, f32[256,512]{1,0:T(8,128)}) custom-call(bf16[256,512]{1,0:T(8,128)(2,1)} %get-tuple-element.21.grad_o, f32[3,256,512]{2,1,0:T(8,128)} %get-tuple-element.20.filtered, bf16[32,16,256]{2,1,0:T(8,128)(2,1)} %copy-done.1, ...), custom_call_target="tpu_custom_call" | custom-call | tf_op jit(solution)/shard_map/back/pallas_call | solution.py:187
  121.7 0.8 convert_element_type.7
  122.5 0.9 broadcast_in_dim.5
  123.4 5.6 %all-to-all-start.4 = ((bf16[32,16,512]{2,1,0:T(8,128)(2,1)}), bf16[32,16,512]{2,1,0:T(8,128)(2,1)S(1)}, u32[]{:S(2)}, u32[]{:S(2)}) async-start(bf16[32,16,512]{2,1,0:T(8,128)(2,1)} %broadcast_in_dim.5), calls=%async_computation.4 | async-start | bytes 1048576 | tf_op jit(solution)/shard_map/all_to_all | solution.py:202
  128.9 2.8 %collective-permute-start.1 = (f32[3,8,512]{2,1,0:T(8,128)}, f32[3,8,512]{2,1,0:T(8,128)S(1)}, u32[]{:S(2)}, u32[]{:S(2)}) collective-permute-start(f32[3,8,512]{2,1,0:T(8,128)} %get-tuple-element.28), channel_id=1, source_target_pairs={{8,0},{16,8},{24,16},{32,24},{40,32},{48,40},{56,48},{64,56},{72,6... | collective-permute-start | bytes 147464 | tf_op jit(solution)/shard_map/ppermute | solution.py:198
  131.7 9.7 %collective-permute-done.1.after = f32[3,8,512]{2,1,0:T(8,128)S(1)} collective-permute-done((f32[3,8,512]{2,1,0:T(8,128)}, f32[3,8,512]{2,1,0:T(8,128)S(1)}, u32[]{:S(2)}, u32[]{:S(2)}) %collective-permute-start.1) | collective-permute-done | bytes 49184 | tf_op jit(solution)/shard_map/ppermute | solution.py:198
  141.4 0.0 copy-start.3
  141.4 0.6 copy-done.3
  142.0 3.0 %taps.1 = (bf16[256,512]{1,0:T(8,128)(2,1)}, bf16[256,512]{1,0:T(8,128)(2,1)}, bf16[256,512]{1,0:T(8,128)(2,1)}) custom-call(f32[3,256,512]{2,1,0:T(8,128)} %get-tuple-element.27.grads, f32[3,8,512]{2,1,0:T(8,128)} %copy-done.3, f32[3,3,512]{2,1,0:T(4,128)} %short.3), custom_call_target="tpu_custom_call" | custom-call | tf_op jit(solution)/shard_map/taps/pallas_call | solution.py:187
  145.0 0.0 all-to-all-done.4
  145.0 0.1 convert_reduce_fusion
  145.1 0.6 slice.21
  145.7 0.6 reshape.16
  (1 shorter events, 0.0 us)
Async XLA Ops:
  7.2 40.1 %all-gather.3.cloned.1.call-start = ((), (), s32[]{:S(2)}) async-start(), calls=%async_computation.5 | async-start | bytes 4718592 | tf_op jit(solution)/shard_map/all_gather | solution.py:211
  9.3 5.5 %collective-permute-start = (bf16[3,2,512]{2,1,0:T(2,128)(2,1)S(1)}, bf16[3,2,512]{2,1,0:T(2,128)(2,1)S(1)}, u32[]{:S(2)}, u32[]{:S(2)}) collective-permute-start(bf16[3,2,512]{2,1,0:T(2,128)(2,1)S(1)} %pad_maximum_fusion), channel_id=1, source_target_pairs={{0,8},{8,16},{16,24},{24,32},{32,40},{40,48},{48,56},{56,64},{64,7... | collective-permute-start | bytes 18440 | tf_op jit(solution)/shard_map/ppermute | solution.py:198
  18.8 38.0 %all-to-all-start = ((bf16[32,2,16,256]{3,2,1,0:T(8,128)(2,1)}), bf16[32,2,16,256]{3,2,1,0:T(8,128)(2,1)S(1)}, u32[]{:S(2)}, u32[]{:S(2)}) async-start(bf16[32,2,16,256]{3,2,1,0:T(8,128)(2,1)} %get-tuple-element.22), calls=%async_computation | async-start | bytes 1048576 | tf_op jit(solution)/shard_map/all_to_all | solution.py:202
  56.8 10.1 %copy-start = (bf16[32,2,16,256]{3,2,1,0:T(8,128)(2,1)}, bf16[32,2,16,256]{3,2,1,0:T(8,128)(2,1)S(1)}, u32[]{:S(2)}) copy-start(bf16[32,2,16,256]{3,2,1,0:T(8,128)(2,1)S(1)} %all-to-all-done.moved) | copy-start | bytes 1572868
  56.8 21.8 %all-to-all-start.2 = ((bf16[32,16,256]{2,1,0:T(8,128)(2,1)}), bf16[32,16,256]{2,1,0:T(8,128)(2,1)S(1)}, u32[]{:S(2)}, u32[]{:S(2)}) async-start(bf16[32,16,256]{2,1,0:T(8,128)(2,1)} %get-tuple-element.24), calls=%async_computation.2 | async-start | bytes 524288 | tf_op jit(solution)/shard_map/all_to_all | solution.py:202
  78.6 5.6 %copy-start.2 = (bf16[32,16,256]{2,1,0:T(8,128)(2,1)}, bf16[32,16,256]{2,1,0:T(8,128)(2,1)S(1)}, u32[]{:S(2)}) copy-start(bf16[32,16,256]{2,1,0:T(8,128)(2,1)S(1)} %all-to-all-done.2.moved) | copy-start | bytes 786436
  78.6 16.2 %all-to-all-start.1 = ((bf16[32,16,256]{2,1,0:T(8,128)(2,1)}), bf16[32,16,256]{2,1,0:T(8,128)(2,1)S(1)}, u32[]{:S(2)}, u32[]{:S(2)}) async-start(bf16[32,16,256]{2,1,0:T(8,128)(2,1)} %get-tuple-element.23), calls=%async_computation.1 | async-start | bytes 524288 | tf_op jit(solution)/shard_map/all_to_all | solution.py:202
  94.8 22.6 %copy-start.1 = (bf16[32,16,256]{2,1,0:T(8,128)(2,1)}, bf16[32,16,256]{2,1,0:T(8,128)(2,1)S(1)}, u32[]{:S(2)}) copy-start(bf16[32,16,256]{2,1,0:T(8,128)(2,1)S(1)} %all-to-all-done.1.conv_y) | copy-start | bytes 786436
  123.4 21.7 %all-to-all-start.4 = ((bf16[32,16,512]{2,1,0:T(8,128)(2,1)}), bf16[32,16,512]{2,1,0:T(8,128)(2,1)S(1)}, u32[]{:S(2)}, u32[]{:S(2)}) async-start(bf16[32,16,512]{2,1,0:T(8,128)(2,1)} %broadcast_in_dim.5), calls=%async_computation.4 | async-start | bytes 1048576 | tf_op jit(solution)/shard_map/all_to_all | solution.py:202
  128.9 12.4 %collective-permute-start.1 = (f32[3,8,512]{2,1,0:T(8,128)}, f32[3,8,512]{2,1,0:T(8,128)S(1)}, u32[]{:S(2)}, u32[]{:S(2)}) collective-permute-start(f32[3,8,512]{2,1,0:T(8,128)} %get-tuple-element.28), channel_id=1, source_target_pairs={{8,0},{16,8},{24,16},{32,24},{40,32},{48,40},{56,48},{64,56},{72,6... | collective-permute-start | bytes 147464 | tf_op jit(solution)/shard_map/ppermute | solution.py:198
  141.4 0.6 copy-start.3
Sparse Core Ops, SparseCore 0:
  9.9 37.3 all-gather.2

commit v2 on v1

v2 whole, which is shorter than its diff:
```python
import functools
import math

import jax
import jax.numpy as jnp
import numpy as np
from jax import lax
from jax.experimental import pallas as pl
from jax.experimental.pallas import tpu as pltpu
from jax.sharding import Mesh, PartitionSpec as P

F32 = jnp.float32
BF16 = jnp.bfloat16
CTX = ("z", "y")
CH = ("x", "core")
SHARDS = 32
ROWS = 256
GROUP = 16
HALF = 8
WIDTH = 512
LENGTH = SHARDS * ROWS
MIB = 1024 * 1024


def halves(table):
    high = table.astype(np.float32).astype(jnp.bfloat16)
    low = (table - high.astype(np.float64)).astype(np.float32).astype(jnp.bfloat16)
    return np.asarray(high), np.asarray(low)


def tables():
    coarse = np.arange(SHARDS)
    angle = 2.0 * math.pi * ((np.outer(4 * coarse + 1, coarse) % (4 * SHARDS)) / (4.0 * SHARDS))
    same = np.eye(HALF)
    spread = np.concatenate([np.kron(np.cos(angle), same), np.kron(-np.sin(angle), same)], axis=0)
    fine = np.arange(ROWS)
    angle = 2.0 * math.pi * ((np.outer(fine, fine) % ROWS) / ROWS)
    cos, sin = np.cos(angle), np.sin(angle)
    turn = np.block([[cos, -sin], [sin, cos]])
    twist = 2.0 * math.pi * np.outer(4 * coarse + 1, fine) / (4.0 * LENGTH)
    twist = np.stack([np.cos(twist), np.sin(twist)])[:, :, None].astype(np.float32)
    return (*halves(spread), *halves(spread.T / LENGTH), *halves(turn), twist)


def dot(left, right):
    return lax.dot_general(left, right, (((1,), (0,)), ((), ())), preferred_element_type=F32)


def split(value):
    high = value.astype(BF16)
    return high, (value - high.astype(F32)).astype(BF16)


def forward(parts, exact, sh, sl, vh, vl, th, tl, twist):
    rows = SHARDS * HALF
    turned = []
    for part in parts:
        high, low = split(part.reshape(rows, ROWS))
        first = dot(sh[...], high) + dot(sl[...], high)
        if not exact:
            first = first + dot(sh[...], low)
        real, imag = [first[i * rows : (i + 1) * rows].reshape(SHARDS, HALF, ROWS) for i in (0, 1)]
        turned.append(
            jnp.concatenate(
                [
                    (real * twist[0] + imag * twist[1]).reshape(rows, ROWS),
                    (imag * twist[0] - real * twist[1]).reshape(rows, ROWS),
                ],
                axis=1,
            )
        )
    high, low = split(jnp.concatenate(turned, axis=0))
    return dot(high, th[...]) + dot(low, th[...]) + dot(high, tl[...])


def inverse(real, imag, sh, sl, vh, vl, th, tl, twist):
    high, low = split(jnp.concatenate([real, -imag], axis=1))
    back = dot(high, th[...]) + dot(low, th[...]) + dot(high, tl[...])
    rows = SHARDS * HALF
    outs = []
    for g in range(2):
        real, minus = [
            back[g * rows : (g + 1) * rows, i * ROWS : (i + 1) * ROWS].reshape(SHARDS, HALF, ROWS)
            for i in (0, 1)
        ]
        high, low = split(
            jnp.concatenate(
                [
                    (real * twist[0] + minus * twist[1]).reshape(rows, ROWS),
                    (real * twist[1] - minus * twist[0]).reshape(rows, ROWS),
                ],
                axis=0,
            )
        )
        out = dot(vh[...], high) + dot(vh[...], low) + dot(vl[...], high)
        outs.append(out.reshape(SHARDS, HALF, ROWS))
    return outs


def turned_lanes(part, amount):
    flat = pltpu.roll(part.reshape(SHARDS * HALF, ROWS), amount, axis=1)
    return flat.reshape(SHARDS, HALF, ROWS)


def lane(part):
    return lax.broadcasted_iota(jnp.int32, part.shape, part.ndim - 1)


def earlier(part, j):
    turned = turned_lanes(part, j)
    before = jnp.concatenate([jnp.zeros((1, HALF, ROWS), F32), turned[:-1]], axis=0)
    return jnp.where(lane(part) < j, before, turned)


def later(part, j):
    turned = turned_lanes(part, ROWS - j)
    behind = jnp.concatenate([turned[1:], jnp.zeros((1, HALF, ROWS), F32)], axis=0)
    return jnp.where(lane(part) >= ROWS - j, behind, turned)


def channels(moved, i, g):
    part = moved[:, i] if i is not None else moved[...]
    return part.astype(F32).reshape(SHARDS, 2, HALF, ROWS)[:, g]


def conv_kernel(*refs):
    moved, lines, *table, spec_mix, spec_fil, y_full, queries, keys, values = refs
    for g in range(2):
        group = slice(HALF * g, HALF * (g + 1))
        for s in range(3):
            part = channels(moved, s, g)
            total = lines[3 * s, group] * part
            for j in (1, 2):
                total = total + lines[3 * s + j, group] * earlier(part, j)
            (queries, keys, values)[s][g] = total
    for out in (queries, keys, values):
        out.start()
    mix = forward([keys[g] * values[g] for g in range(2)], False, *table)
    fil = forward([channels(moved, 3, g) for g in range(2)], True, *table)
    spec_mix[...] = mix
    spec_mix.start()
    spec_fil[...] = fil
    spec_fil.start()
    mix_re, mix_im = mix[:, :ROWS], mix[:, ROWS:]
    fil_re, fil_im = fil[:, :ROWS], fil[:, ROWS:]
    conv_y = inverse(
        mix_re * fil_re - mix_im * fil_im, mix_re * fil_im + mix_im * fil_re, *table
    )
    for g in range(2):
        group = slice(HALF * g, HALF * (g + 1))
        y_full[g] = conv_y[g] + lines[9, group] * (keys[g] * values[g])


def grad_kernel(*refs):
    grad_moved, queries, *table, spec_mix, spec_fil, y_full, lines, moved, keys, values, out, kept = (
        refs
    )
    grad_y = [channels(grad_moved, None, g) * queries[g] for g in range(2)]
    grad = forward(grad_y, False, *table)
    grad_re, grad_im = grad[:, :ROWS], grad[:, ROWS:]

    def correlate(spec):
        re, im = spec[:, :ROWS], spec[:, ROWS:]
        return inverse(grad_re * re + grad_im * im, grad_im * re - grad_re * im, *table)

    def put(i, parts):
        both = jnp.concatenate(parts, axis=1).astype(BF16)
        out[:, 32 * i : 32 * i + 16, :] = both[:, :, :128]
        out[:, 32 * i + 16 : 32 * i + 32, :] = both[:, :, 128:]

    put(3, correlate(spec_mix))
    conv_back = correlate(spec_fil)
    place = lax.broadcasted_iota(jnp.int32, (HALF, 128), 1)
    sums = jnp.zeros((HALF, 128), F32)
    for s in range(3):
        for g in range(2):
            group = slice(HALF * g, HALF * (g + 1))
            if s == 0:
                part = channels(grad_moved, None, g) * y_full[g]
            else:
                part = (conv_back[g] + lines[9, group] * grad_y[g]) * (values, keys)[s - 1][g]
            stream = channels(moved, s, g)
            total = jnp.zeros_like(part)
            for j in range(3):
                ahead = later(part, j) if j else part
                total = total + lines[3 * s + j, group] * ahead
                term = jnp.sum(jnp.sum(ahead * stream, axis=0), axis=1, keepdims=True)
                sums = jnp.where(place == 10 * g + 3 * s + j, term, sums)
            kept[g] = total
        put(s, [kept[0], kept[1]])
    for g in range(2):
        term = jnp.sum(
            jnp.sum(grad_y[g] * (keys[g] * values[g]), axis=0), axis=1, keepdims=True
        )
        sums = jnp.where(place == 10 * g + 9, term, sums)
    high = sums.astype(BF16).astype(F32)
    sums = high + pltpu.roll(sums - high, 64, axis=1)
    out[:, 128:136, :] = jnp.broadcast_to(sums[None], (SHARDS, HALF, 128)).astype(BF16)


def pack_kernel(queries, keys, values, long_filter, send):
    for s, stream in enumerate((queries, keys, values, long_filter)):
        send[:, s] = stream[...].astype(F32).T.reshape(SHARDS, GROUP, ROWS).astype(BF16)


def unpack_kernel(moved, d_queries, d_keys, d_values, d_long, d_short, d_skip):
    for i, out in enumerate((d_queries, d_keys, d_values, d_long)):
        for half in range(2):
            start = 32 * i + 16 * half
            part = moved[:, start : start + 16, :].astype(F32).reshape(WIDTH, 128)
            out[128 * half : 128 * (half + 1), :] = part.T.astype(out.dtype)
    sums = moved[:, 128:136, :].astype(F32).reshape(SHARDS * HALF, 128).T
    source = lax.broadcasted_iota(jnp.int32, (SHARDS * HALF, WIDTH), 0)
    target = lax.broadcasted_iota(jnp.int32, (SHARDS * HALF, WIDTH), 1)
    totals = jnp.zeros((10, WIDTH), F32)
    for g in range(2):
        aim = source + (source // HALF) * HALF + HALF * g
        place = (target == aim).astype(F32).astype(BF16)
        spread = dot(sums.astype(BF16), place)
        totals = totals + spread[10 * g : 10 * g + 10] + spread[64 + 10 * g : 64 + 10 * g + 10]
    for s in range(3):
        d_short[s] = totals[3 * s : 3 * s + 3]
    d_skip[...] = totals[9:10]


def project_kernel(count, at, first, last, *refs):
    blocks, (w_out, order, *rest) = refs[:count], refs[count:]
    held, own, arrived = rest[-3:]
    depth = blocks[0].shape[1]
    if first:
        block = Arriving(blocks[0], own, own, arrived.at[count])
        block.start()
        blocks = [block, *blocks[1:]]
    slices = []
    for i in range(count):
        columns = pl.ds(pl.multiple_of(order[at + i] * depth, depth), depth)
        slices.append(Arriving(w_out.at[:, columns], held.at[i], held.at[i], arrived.at[i]))
        slices[-1].start()
    total = jnp.zeros((WIDTH, ROWS), F32) if first else rest[0][...]
    for i in range(count):
        total = total + lax.dot_general(
            slices[i][...], blocks[i][...], (((1,), (1,)), ((), ())), preferred_element_type=F32
        )
    out = rest[0 if first else 1]
    out[...] = total.astype(BF16).reshape(SHARDS, GROUP, ROWS) if last else total


def project(blocks, at, w_out, order, before=None, last=False):
    count = len(blocks)
    depth = blocks[0].shape[1]
    first = before is None
    vmem = pl.BlockSpec(memory_space=pltpu.VMEM)
    anywhere = pl.BlockSpec(memory_space=pl.ANY)
    specs = [anywhere if first and i == 0 else vmem for i in range(count)]
    specs += [anywhere, pl.BlockSpec(memory_space=pltpu.SMEM)] + [vmem] * (not first)
    blocks = [in_hbm(b) if first and i == 0 else in_vmem(b) for i, b in enumerate(blocks)]
    return pl.pallas_call(
        functools.partial(project_kernel, count, at, first, last),
        out_shape=shape((SHARDS, GROUP, ROWS), BF16) if last else shape((WIDTH, ROWS)),
        in_specs=specs,
        out_specs=vmem,
        scratch_shapes=[
            pltpu.VMEM((count, WIDTH, depth), BF16),
            pltpu.VMEM((ROWS, depth), BF16),
            pltpu.SemaphoreType.DMA((count + 1,)),
        ],
        compiler_params=pltpu.CompilerParams(vmem_limit_bytes=12 * MIB),
        cost_estimate=pl.CostEstimate(
            flops=2 * count * ROWS * depth * WIDTH,
            bytes_accessed=2 * count * WIDTH * depth,
            transcendentals=0,
        ),
        name="project",
    )(*blocks, in_hbm(w_out), order, *([] if first else [in_vmem(before)]))


def in_vmem(array):
    return pltpu.with_memory_space_constraint(array, pltpu.VMEM)


def in_hbm(array):
    return pltpu.with_memory_space_constraint(array, pltpu.HBM)


class Moving:
    def __init__(self, source, target, held, done):
        self.copy, self.held = pltpu.make_async_copy(source, target, done), held
        self.started = self.ended = False
        self.dtype = held.dtype

    def start(self):
        if not self.started:
            self.copy.start()
            self.started = True

    def wait(self):
        self.start()
        if not self.ended:
            self.copy.wait()
            self.ended = True


class Arriving(Moving):
    behind = ()

    def __getitem__(self, index):
        self.wait()
        for array in self.behind:
            array.start()
        return self.held[index]


class Leaving(Moving):
    def __getitem__(self, index):
        return self.held[index]

    def __setitem__(self, index, value):
        self.held[index] = value


def staged_kernel(kernel, count, outs, urgent, *refs):
    sources, targets, refs = refs[:count], refs[count : count + outs], refs[count + outs :]
    held, built = refs[:count], refs[count:]
    built, (*scratch, arrived, sent) = built[:outs], built[outs:]
    arriving = [Arriving(sources[i], held[i], held[i], arrived.at[i]) for i in range(count)]
    leaving = [Leaving(built[i], targets[i], built[i], sent.at[i]) for i in range(outs)]
    for array in arriving[:urgent]:
        array.start()
    arriving[urgent - 1].behind = arriving[urgent:]
    kernel(*arriving, *leaving, *scratch)
    for array in (*arriving, *leaving):
        array.start()
    for array in (*arriving, *leaving):
        array.wait()


def call(
    kernel, out_shape, *args, scratch=(), name, limit=12, flops=0, moved=4 * MIB, urgent=None
):
    count, outs = len(args), len(out_shape)
    anywhere = pl.BlockSpec(memory_space=pl.ANY)
    return pl.pallas_call(
        functools.partial(staged_kernel, kernel, count, outs, urgent or count),
        out_shape=out_shape,
        in_specs=[anywhere] * count,
        out_specs=tuple([anywhere] * outs),
        scratch_shapes=(
            *[pltpu.VMEM(arg.shape, arg.dtype) for arg in args],
            *[pltpu.VMEM(out.shape, out.dtype) for out in out_shape],
            *scratch,
            pltpu.SemaphoreType.DMA((count,)),
            pltpu.SemaphoreType.DMA((outs,)),
        ),
        compiler_params=pltpu.CompilerParams(vmem_limit_bytes=limit * MIB),
        cost_estimate=pl.CostEstimate(flops=flops, bytes_accessed=moved, transcendentals=0),
        name=name,
    )(*args)


def exchange(blocks):
    return lax.all_to_all(blocks, CTX, split_axis=0, concat_axis=0, tiled=True)


def shape(dims, dtype=F32):
    return jax.ShapeDtypeStruct(dims, dtype)


def gathered_product(d_out, w_out):
    x_size = lax.axis_size("x")
    x, core = lax.axis_index("x"), lax.axis_index("core")
    near, far = (x + 2 * core - 1) % x_size, (x + 2) % x_size
    other_near = (x + 1 - 2 * core) % x_size
    order = jnp.stack(
        [
            2 * x + core, 2 * x + 1 - core,
            2 * near + core, 2 * other_near + 1 - core,
            2 * near + 1 - core, 2 * other_near + core,
            2 * far + core, 2 * far + 1 - core,
        ]
    ).astype(jnp.int32)
    first, sibling = ahead(d_out), swap(d_out)
    total = project([d_out, sibling], 0, w_out, order)
    second = ahead(sibling)
    third = ahead(first)
    first_other = swap(first)
    second, total = lax.optimization_barrier((second, total))
    second_other = swap(second)
    total = project([first, first_other], 2, w_out, order, total)
    third, total = lax.optimization_barrier((third, total))
    third_other = swap(third)
    total = project([second, second_other], 4, w_out, order, total)
    return project([third, third_other], 6, w_out, order, total, last=True)


def swap(block):
    return lax.ppermute(block, CH, [(i, i ^ 1) for i in range(2 * lax.axis_size("x"))])


def ahead(block):
    size = lax.axis_size("x")
    route = [(2 * i + c, 2 * ((i + 1 - 2 * c) % size) + c) for i in range(size) for c in range(2)]
    return lax.ppermute(block, CH, route)


def per_device(queries, keys, values, long_filter, short, skip, w_out, d_out):
    (send,) = call(
        pack_kernel,
        (shape((SHARDS, 4, GROUP, ROWS), BF16),),
        *[in_hbm(stream) for stream in (queries, keys, values, long_filter)],
        name="pack",
    )
    moved = in_hbm(exchange(send))
    mine = lax.axis_index(CTX) * GROUP
    lines = jnp.concatenate([short.reshape(9, WIDTH), skip[None]], axis=0)
    lines = lax.dynamic_slice(lines, (0, mine), (10, GROUP))
    lines = jnp.broadcast_to(lines[:, :, None], (10, GROUP, ROWS))
    table = [in_hbm(jnp.asarray(array)) for array in tables()]
    grad_moved = exchange(gathered_product(d_out, w_out))
    spec = pltpu.HBM((2 * SHARDS * HALF, 2 * ROWS), F32)
    part = pltpu.HBM((2, SHARDS, HALF, ROWS), F32)
    transform = 2 * 600 * MIB
    kept = call(
        conv_kernel,
        (spec, spec, part, part, part, part),
        moved, lines, *table,
        name="conv", limit=40, flops=3 * transform, urgent=2,
    )
    spec_mix, spec_fil, y_full, *filtered = [in_hbm(array) for array in kept]
    (back,) = call(
        grad_kernel,
        (shape((SHARDS, 136, 128), BF16),),
        grad_moved, filtered[0], *table, spec_mix, spec_fil, y_full, lines, moved, *filtered[1:],
        scratch=(pltpu.VMEM((2, SHARDS, HALF, ROWS), F32),),
        name="grad_conv", limit=40, flops=3 * transform, urgent=2,
    )
    stream = shape((ROWS, WIDTH), BF16)
    *grads, d_short, d_skip = call(
        unpack_kernel,
        (stream, stream, stream, shape((ROWS, WIDTH)), shape((3, 3, WIDTH)), shape((1, WIDTH))),
        exchange(back),
        name="unpack", limit=16,
    )
    return *grads, d_short, d_skip[0]


def solution(mesh):
    fine_mesh = Mesh(mesh.devices.reshape(8, 4, 4, 2), ("z", "y", "x", "core"))
    block = P(CTX, CH)
    in_specs = (block, block, block, block, P(None, None, CH), P(CH), P(CH, None), block)
    out_specs = (block, block, block, block, P(None, None, CH), P(CH))
    return jax.shard_map(
        per_device, mesh=fine_mesh, in_specs=in_specs, out_specs=out_specs, check_vma=False
    )
```

time: 154 us -> 115 us (0.75)
  waiting for transfers between devices: 36.4 us -> 15.3 us
  starting transfers between devices: 39.7 us -> 24.9 us
  blocking collectives: 22.6 us -> 36.5 us
  between operations: 14.1 us -> 0.96 us
  local copies, waits for them, and re-layouts: 4.14 us -> 0.2 us
    all_gather x1 -> x0, waiting for transfers between devices: 16.3 us -> none  [per_device(): gathered = lax.all_gather(d_out, CH, axis=0, tiled=False)]
    all_to_all x1, blocking collectives: 22.6 us -> 36.5 us  [exchange(): return lax.all_to_all(blocks, CTX, split_axis=0, concat_axis=0, tiled=True)]
    all_to_all x4 -> x2, starting transfers between devices: 33.4 us -> 21.5 us  [exchange(): return lax.all_to_all(blocks, CTX, split_axis=0, concat_axis=0, tiled=True)]
    all_to_all x4 -> x2, waiting for transfers between devices: 7.71 us -> 3.29 us  [exchange(): return lax.all_to_all(blocks, CTX, split_axis=0, concat_axis=0, tiled=True)]
    ppermute x2 -> x7, starting transfers between devices: 6.25 us -> 3.44 us  [the longest x3 3.34 us: ahead(): return lax.ppermute(block, CH, route)]
    pallas_call x6 -> x8, Pallas kernels: 34.8 us -> 36.1 us  [the longest x4 22.6 us: call(): pl.pallas_call(functools.partial(staged_kernel, kernel, count, outs, urge...]
    ppermute x2 -> x7, waiting for transfers between devices: 11.7 us -> 12 us  [the longest x3 11.7 us: ahead(): return lax.ppermute(block, CH, route)]
  transfers between devices with their start and end apart: 7 -> 9, of which waited for: 5 -> 5; matrix products, arithmetic and copies ran while one was open for 1% -> 0% of each run, Pallas kernels for 20% -> 19%
where the time goes in v2:
time: 115 us; the launch traced here: 114 us
  blocking collectives  36.5 us (32%)
  Pallas kernels  36.1 us (31%)
  starting transfers between devices  24.9 us (22%)
  waiting for transfers between devices  15.3 us (13%)
    all_to_all x1, blocking collectives, exchange(): return lax.all_to_all(blocks, CTX, split_axis=0, concat_axis=0, tiled=True)  36.5 us
    pallas_call x4, Pallas kernels, call(): pl.pallas_call(functools.partial(staged_kernel, kernel, count, outs, urge...  22.6 us
    all_to_all x2, starting transfers between devices, exchange(): return lax.all_to_all(blocks, CTX, split_axis=0, concat_axis=0, tiled=True)  21.5 us
    pallas_call x4, Pallas kernels, project(): pl.pallas_call(functools.partial(project_kernel, count, at, first, last),...  13.5 us
    ppermute x3, waiting for transfers between devices, ahead(): return lax.ppermute(block, CH, route)  11.7 us
    ppermute x3, starting transfers between devices, ahead(): return lax.ppermute(block, CH, route)  3.34 us
    all_to_all x2, waiting for transfers between devices, exchange(): return lax.all_to_all(blocks, CTX, split_axis=0, concat_axis=0, tiled=True)  3.29 us
  transfers between devices with their start and end apart: 9, of which 5 were waited for; matrix products, arithmetic and copies ran while one was open for 0% of the time, Pallas kernels for 19%

profile of v2, /device:TPU:24, one launch (start us, length us, event | category | flops | bytes accessed | tf_op | source)
XLA Modules:
  0.0 114.0 jit_solution(16624498906932800593)
XLA Ops:
  0.6 2.5 %pack.1 = bf16[32,4,16,256]{3,2,1,0:T(8,128)(2,1)} custom-call(bf16[256,512]{1,0:T(8,128)(2,1)} %refs_0_.3, bf16[256,512]{1,0:T(8,128)(2,1)} %refs_1_.1, bf16[256,512]{1,0:T(8,128)(2,1)} %refs_2_.11, f32[256,512]{1,0:T(8,128)} %refs_3_.3), custom_call_target="tpu_custom_call" | custom-call | bytes 4194304 | tf_op jit(solution)/shard_map/pack/pallas_call | solution.py:342
  3.2 0.0 copy-start
  3.2 11.7 %all-to-all-start.1 = ((bf16[32,4,16,256]{3,2,1,0:T(8,128)(2,1)}), bf16[32,4,16,256]{3,2,1,0:T(8,128)(2,1)}, u32[]{:S(2)}, u32[]{:S(2)}) async-start(bf16[32,4,16,256]{3,2,1,0:T(8,128)(2,1)} %pack.1), calls=%async_computation.1 | async-start | bytes 2097152 | tf_op jit(solution)/shard_map/all_to_all | solution.py:361
  14.9 0.0 copy-done
  14.9 0.1 collective-permute-start.3
  15.0 1.6 %collective-permute-start = (bf16[256,1024]{1,0:T(8,128)(2,1)S(1)}, bf16[256,1024]{1,0:T(8,128)(2,1)S(1)}, u32[]{:S(2)}, u32[]{:S(2)}) collective-permute-start(bf16[256,1024]{1,0:T(8,128)(2,1)S(1)} %copy-done), channel_id=1, source_target_pairs={{0,2},{1,7},{2,4},{3,1},{4,6},{5,3},{6,0},{7,5},{8,10},{9,15},{10,... | collective-permute-start | bytes 1572872 | tf_op jit(solution)/shard_map/ppermute | solution.py:402
  16.6 0.3 collective-permute-done.3.refs_1_
  16.9 1.5 %collective-permute-start.4 = (bf16[256,1024]{1,0:T(8,128)(2,1)S(1)}, bf16[256,1024]{1,0:T(8,128)(2,1)S(1)}, u32[]{:S(2)}, u32[]{:S(2)}) collective-permute-start(bf16[256,1024]{1,0:T(8,128)(2,1)S(1)} %collective-permute-done.3.refs_1_), channel_id=1, source_target_pairs={{0,2},{1,7},{2,4},{3,1},{4,6},{5,3},{6,0},{7,5},{8,10},{9,15},{10,... | collective-permute-start | bytes 1572872 | tf_op jit(solution)/shard_map/ppermute | solution.py:402
  18.4 7.1 %collective-permute-done.refs_0_ = bf16[256,1024]{1,0:T(8,128)(2,1)S(1)} collective-permute-done((bf16[256,1024]{1,0:T(8,128)(2,1)S(1)}, bf16[256,1024]{1,0:T(8,128)(2,1)S(1)}, u32[]{:S(2)}, u32[]{:S(2)}) %collective-permute-start) | collective-permute-done | bytes 524320 | tf_op jit(solution)/shard_map/ppermute | solution.py:402
  25.5 0.0 collective-permute-start.2
  25.5 0.3 collective-permute-start.1
  25.7 0.1 stack.35.refs_3_
  25.8 3.0 %project.4.refs_4_ = f32[512,256]{1,0:T(8,128)S(1)} custom-call(bf16[256,1024]{1,0:T(8,128)(2,1)} %refs_0_.2, bf16[256,1024]{1,0:T(8,128)(2,1)S(1)} %collective-permute-done.3.refs_1_, bf16[512,8192]{1,0:T(8,128)(2,1)} %refs_2_.10, s32[8]{0:T(128)S(1)} %stack.35.refs_3_), custom_call_target="tpu_custom_call" | custom-call | flops 536870912 | bytes 2097152 | tf_op jit(solution)/shard_map/project/pallas_call | solution.py:257
  28.8 2.2 %collective-permute-done.4.refs_0_ = bf16[256,1024]{1,0:T(8,128)(2,1)S(1)} collective-permute-done((bf16[256,1024]{1,0:T(8,128)(2,1)S(1)}, bf16[256,1024]{1,0:T(8,128)(2,1)S(1)}, u32[]{:S(2)}, u32[]{:S(2)}) %collective-permute-start.4) | collective-permute-done | bytes 524320 | tf_op jit(solution)/shard_map/ppermute | solution.py:402
  31.1 0.0 collective-permute-start.6
  31.1 0.0 collective-permute-done.2.refs_1_
  31.1 3.2 %project.5.refs_4_ = f32[512,256]{1,0:T(8,128)S(1)} custom-call(bf16[256,1024]{1,0:T(8,128)(2,1)S(1)} %collective-permute-done.refs_0_, bf16[256,1024]{1,0:T(8,128)(2,1)S(1)} %collective-permute-done.2.refs_1_, bf16[512,8192]{1,0:T(8,128)(2,1)} %refs_2_.10, s32[8]{0:T(128)S(1)} %stack.35.refs_3_, f32[512,256]{1,0:T(8,128)S(1)} %project.4.refs_4_), custom_call_target="tpu_custom_call" | custom-call | flops 536870912 | bytes 2097152 | tf_op jit(solution)/shard_map/project/pallas_call | solution.py:257
  34.3 2.4 %collective-permute-done.1.refs_0_ = bf16[256,1024]{1,0:T(8,128)(2,1)S(1)} collective-permute-done((bf16[256,1024]{1,0:T(8,128)(2,1)S(1)}, bf16[256,1024]{1,0:T(8,128)(2,1)S(1)}, u32[]{:S(2)}, u32[]{:S(2)}) %collective-permute-start.1) | collective-permute-done | bytes 524320 | tf_op jit(solution)/shard_map/ppermute | solution.py:402
  36.7 0.0 collective-permute-start.5
  36.7 0.0 collective-permute-done.6.refs_1_
  36.7 3.2 %project.6.refs_4_ = f32[512,256]{1,0:T(8,128)S(1)} custom-call(bf16[256,1024]{1,0:T(8,128)(2,1)S(1)} %collective-permute-done.4.refs_0_, bf16[256,1024]{1,0:T(8,128)(2,1)S(1)} %collective-permute-done.6.refs_1_, bf16[512,8192]{1,0:T(8,128)(2,1)} %refs_2_.10, s32[8]{0:T(128)S(1)} %stack.35.refs_3_, f32[512,256]{1,0:T(8,128)S(1)} %project.5.refs_4_), custom_call_target="tpu_custom_call" | custom-call | flops 536870912 | bytes 2097152 | tf_op jit(solution)/shard_map/project/pallas_call | solution.py:257
  39.9 0.0 copy-start.1
  40.0 0.0 copy-start.2
  40.0 0.0 collective-permute-done.5.refs_1_
  40.0 3.9 %project.7 = bf16[32,16,256]{2,1,0:T(8,128)(2,1)} custom-call(bf16[256,1024]{1,0:T(8,128)(2,1)S(1)} %collective-permute-done.1.refs_0_, bf16[256,1024]{1,0:T(8,128)(2,1)S(1)} %collective-permute-done.5.refs_1_, bf16[512,8192]{1,0:T(8,128)(2,1)} %refs_2_.10, s32[8]{0:T(128)S(1)} %stack.35.refs_3_, f32[512,256]{1,0:T(8,128)S(1)} %project.6.refs_4_), custom_call_target="tpu_custom_call" | custom-call | flops 536870912 | bytes 2097152 | tf_op jit(solution)/shard_map/project/pallas_call | solution.py:257
  43.9 0.0 all-to-all-done.1.refs_0_.refs_13_
  43.9 9.8 %all-to-all-start = ((bf16[32,16,256]{2,1,0:T(8,128)(2,1)}), bf16[32,16,256]{2,1,0:T(8,128)(2,1)S(1)}, u32[]{:S(2)}, u32[]{:S(2)}) async-start(bf16[32,16,256]{2,1,0:T(8,128)(2,1)} %project.7), calls=%async_computation | async-start | bytes 524288 | tf_op jit(solution)/shard_map/all_to_all | solution.py:361
  53.8 0.0 copy-done.1
  53.8 0.0 copy-done.2
  53.8 0.1 fusion
  53.9 0.1 broadcast_in_dim.10.refs_1_.refs_12_
  54.0 8.4 %conv.1 = (f32[512,512]{1,0:T(8,128)}, f32[512,512]{1,0:T(8,128)}, f32[2,32,8,256]{3,2,1,0:T(8,128)}, f32[2,32,8,256]{3,2,1,0:T(8,128)}, f32[2,32,8,256]{3,2,1,0:T(8,128)}, /*index=5*/f32[2,32,8,256]{3,2,1,0:T(8,128)}) custom-call(bf16[32,4,16,256]{3,2,1,0:T(8,128)(2,1)} %all-to-all-done.1.refs_0_.refs_13_, ...), custom_call_target="tpu_custom_call" | custom-call | flops 3774873600 | bytes 4194304 | tf_op jit(solution)/shard_map/conv/pallas_call | solution.py:342
  62.3 3.3 %all-to-all-done.refs_0_ = bf16[32,16,256]{2,1,0:T(8,128)(2,1)S(1)} async-done(((bf16[32,16,256]{2,1,0:T(8,128)(2,1)}), bf16[32,16,256]{2,1,0:T(8,128)(2,1)S(1)}, u32[]{:S(2)}, u32[]{:S(2)}) %all-to-all-start) | async-done | bytes 262176 | tf_op jit(solution)/shard_map/all_to_all | solution.py:361
  65.6 10.2 %grad_conv.1 = bf16[32,136,128]{2,1,0:T(8,128)(2,1)S(1)} custom-call(bf16[32,16,256]{2,1,0:T(8,128)(2,1)S(1)} %all-to-all-done.refs_0_, f32[2,32,8,256]{3,2,1,0:T(8,128)} %get-tuple-element.26.refs_1_, bf16[512,256]{1,0:T(8,128)(2,1)} %constant.62.clone.refs_2_, bf16[512,256]{1,0:T(8,128)(2,1)} %constant.63.clone.refs_3_, ...), custom_call_target="tpu_custom_call" | custom-call | flops 3774873600 | bytes 4194304 | tf_op jit(solution)/shard_map/grad_conv/pallas_call | solution.py:342
  75.8 36.5 %all_to_all.15.refs_0_ = bf16[32,136,128]{2,1,0:T(8,128)(2,1)S(1)} all-to-all(bf16[32,136,128]{2,1,0:T(8,128)(2,1)S(1)} %grad_conv.1), channel_id=1, replica_groups=mesh['z'=8,'y'=4,'x'=4,'core'=2] {'z','y'}, dimensions={0} | all-to-all | bytes 2228224 | tf_op jit(solution)/shard_map/all_to_all | solution.py:361
  112.3 1.5 %unpack.1 = (bf16[256,512]{1,0:T(8,128)(2,1)}, bf16[256,512]{1,0:T(8,128)(2,1)}, bf16[256,512]{1,0:T(8,128)(2,1)}, f32[256,512]{1,0:T(8,128)}, f32[3,3,512]{2,1,0:T(4,128)}, /*index=5*/f32[1,512]{1,0:T(1,128)}) custom-call(bf16[32,136,128]{2,1,0:T(8,128)(2,1)S(1)} %all_to_all.15.refs_0_), custom_call_target="tpu_custom_call" | custom-call | bytes 4194304 | tf_op jit(solution)/shard_map/unpack/pallas_call | solution.py:342
  (1 shorter events, 0.0 us)
Async XLA Ops:
  3.2 11.7 %copy-start = (bf16[256,1024]{1,0:T(8,128)(2,1)S(1)}, bf16[256,1024]{1,0:T(8,128)(2,1)}, u32[]{:S(2)}) copy-start(bf16[256,1024]{1,0:T(8,128)(2,1)} %refs_0_.2) | copy-start | bytes 1572868
  3.2 40.7 %all-to-all-start.1 = ((bf16[32,4,16,256]{3,2,1,0:T(8,128)(2,1)}), bf16[32,4,16,256]{3,2,1,0:T(8,128)(2,1)}, u32[]{:S(2)}, u32[]{:S(2)}) async-start(bf16[32,4,16,256]{3,2,1,0:T(8,128)(2,1)} %pack.1), calls=%async_computation.1 | async-start | bytes 2097152 | tf_op jit(solution)/shard_map/all_to_all | solution.py:361
  14.9 2.0 %collective-permute-start.3 = (bf16[256,1024]{1,0:T(8,128)(2,1)S(1)}, bf16[256,1024]{1,0:T(8,128)(2,1)S(1)}, u32[]{:S(2)}, u32[]{:S(2)}) collective-permute-start(bf16[256,1024]{1,0:T(8,128)(2,1)S(1)} %copy-done), channel_id=1, source_target_pairs={{0,1},{1,0},{2,3},{3,2},{4,5},{5,4},{6,7},{7,6},{8,9},{9,8},{10,11... | collective-permute-start | bytes 1572872 | tf_op jit(solution)/shard_map/ppermute | solution.py:396
  15.0 10.5 %collective-permute-start = (bf16[256,1024]{1,0:T(8,128)(2,1)S(1)}, bf16[256,1024]{1,0:T(8,128)(2,1)S(1)}, u32[]{:S(2)}, u32[]{:S(2)}) collective-permute-start(bf16[256,1024]{1,0:T(8,128)(2,1)S(1)} %copy-done), channel_id=1, source_target_pairs={{0,2},{1,7},{2,4},{3,1},{4,6},{5,3},{6,0},{7,5},{8,10},{9,15},{10,... | collective-permute-start | bytes 1572872 | tf_op jit(solution)/shard_map/ppermute | solution.py:402
  16.9 14.2 %collective-permute-start.4 = (bf16[256,1024]{1,0:T(8,128)(2,1)S(1)}, bf16[256,1024]{1,0:T(8,128)(2,1)S(1)}, u32[]{:S(2)}, u32[]{:S(2)}) collective-permute-start(bf16[256,1024]{1,0:T(8,128)(2,1)S(1)} %collective-permute-done.3.refs_1_), channel_id=1, source_target_pairs={{0,2},{1,7},{2,4},{3,1},{4,6},{5,3},{6,0},{7,5},{8,10},{9,15},{10,... | collective-permute-start | bytes 1572872 | tf_op jit(solution)/shard_map/ppermute | solution.py:402
  25.5 5.6 %collective-permute-start.2 = (bf16[256,1024]{1,0:T(8,128)(2,1)S(1)}, bf16[256,1024]{1,0:T(8,128)(2,1)S(1)}, u32[]{:S(2)}, u32[]{:S(2)}) collective-permute-start(bf16[256,1024]{1,0:T(8,128)(2,1)S(1)} %collective-permute-done.refs_0_), channel_id=1, source_target_pairs={{0,1},{1,0},{2,3},{3,2},{4,5},{5,4},{6,7},{7,6},{8,9},{9,8},{10,11... | collective-permute-start | bytes 1572872 | tf_op jit(solution)/shard_map/ppermute | solution.py:396
  25.5 11.2 %collective-permute-start.1 = (bf16[256,1024]{1,0:T(8,128)(2,1)S(1)}, bf16[256,1024]{1,0:T(8,128)(2,1)S(1)}, u32[]{:S(2)}, u32[]{:S(2)}) collective-permute-start(bf16[256,1024]{1,0:T(8,128)(2,1)S(1)} %collective-permute-done.refs_0_), channel_id=1, source_target_pairs={{0,2},{1,7},{2,4},{3,1},{4,6},{5,3},{6,0},{7,5},{8,10},{9,15},{10,... | collective-permute-start | bytes 1572872 | tf_op jit(solution)/shard_map/ppermute | solution.py:402
  31.1 5.6 %collective-permute-start.6 = (bf16[256,1024]{1,0:T(8,128)(2,1)S(1)}, bf16[256,1024]{1,0:T(8,128)(2,1)S(1)}, u32[]{:S(2)}, u32[]{:S(2)}) collective-permute-start(bf16[256,1024]{1,0:T(8,128)(2,1)S(1)} %collective-permute-done.4.refs_0_), channel_id=1, source_target_pairs={{0,1},{1,0},{2,3},{3,2},{4,5},{5,4},{6,7},{7,6},{8,9},{9,8},{10,11... | collective-permute-start | bytes 1572872 | tf_op jit(solution)/shard_map/ppermute | solution.py:396
  36.7 3.3 %collective-permute-start.5 = (bf16[256,1024]{1,0:T(8,128)(2,1)S(1)}, bf16[256,1024]{1,0:T(8,128)(2,1)S(1)}, u32[]{:S(2)}, u32[]{:S(2)}) collective-permute-start(bf16[256,1024]{1,0:T(8,128)(2,1)S(1)} %collective-permute-done.1.refs_0_), channel_id=1, source_target_pairs={{0,1},{1,0},{2,3},{3,2},{4,5},{5,4},{6,7},{7,6},{8,9},{9,8},{10,11... | collective-permute-start | bytes 1572872 | tf_op jit(solution)/shard_map/ppermute | solution.py:396
  39.9 13.8 %copy-start.1 = (f32[3,3,512]{2,1,0:T(4,128)S(1)}, f32[3,3,512]{2,1,0:T(4,128)}, u32[]{:S(2)}) copy-start(f32[3,3,512]{2,1,0:T(4,128)} %param.19) | copy-start | bytes 55300
  40.0 13.8 %copy-start.2 = (f32[512]{0:T(512)S(1)}, f32[512]{0:T(512)}, u32[]{:S(2)}) copy-start(f32[512]{0:T(512)} %param.20) | copy-start | bytes 6148
  43.9 21.7 %all-to-all-start = ((bf16[32,16,256]{2,1,0:T(8,128)(2,1)}), bf16[32,16,256]{2,1,0:T(8,128)(2,1)S(1)}, u32[]{:S(2)}, u32[]{:S(2)}) async-start(bf16[32,16,256]{2,1,0:T(8,128)(2,1)} %project.7), calls=%async_computation | async-start | bytes 524288 | tf_op jit(solution)/shard_map/all_to_all | solution.py:361
